TPU v7x, 512 devices: a whole 4x4x16 slice. The times are simulated.
512 devices in a mesh: tm: 32 (over x, z_lo), space: 16 (over y, z_hi, core).
Axes of the slice: x: 4, y: 4, z: 16 (z_hi: 2, z_lo: 8; z = z_hi * 8 + z_lo), core: 2. Of those that a mesh axis runs over, the one named last changes fastest.
Arguments:
- u_old: float32 [32, 5, 256, 16, 128], P('tm', None, 'space'), may hold values from -2.5 to 2.5
- u_init: float32 [256, 16, 128], P('space'), may hold values from -2.5 to 2.5
Outputs:
- u_new: float32 [32, 5, 256, 16, 128], P('tm', None, 'space')
All inputs are finite; a program needn't handle non-finite values.
Results may differ from a plain program's by a relative error of at most 0.0003.
Values sent between devices are 32-bit elements; how exact they have to be, the bound alone decides.
No kernel may reach another device: no remote copies, remote signals or barrier semaphores. Data moves between devices by JAX's collectives and lax.ppermute only.
A program may use at most 64 MiB of HBM per device.

v0:
```python
import math
import jax
import jax.numpy as jnp
from jax import lax
from jax.sharding import Mesh
from jax.sharding import PartitionSpec as P

SPACE = ("space_0", "space_1", "space_2")
step_length = 0.4
diffusion = 1.0
reaction = 1.0


def passed_along(value, axis, steps):
    count = lax.axis_size(axis)
    leading, last = (max(0, -steps), min(count, count - steps))
    return lax.ppermute(value, axis, [(source, source + steps) for source in range(leading, last)])


def padded_2(x, sides, width):
    for axis, dim in sides:
        count, length = (lax.axis_size(axis), x.shape[dim])
        up = [(i, (i + 1) % count) for i in range(count)]
        down = [(j, i) for i, j in up]
        last = lax.slice_in_dim(x, length - width, length, axis=dim)
        leading = lax.slice_in_dim(x, 0, width, axis=dim)
        before = lax.ppermute(last, axis, up)
        after = lax.ppermute(leading, axis, down)
        x = jnp.concatenate([before, x, after], axis=dim)
    return x


def split_up(x, dim, count):
    before, after = (x.shape[:dim], x.shape[dim + 1 :])
    return jnp.moveaxis(x.reshape(*before, count, -1, *after), dim, 0)


def laid_out(parts, dim):
    parts = jnp.moveaxis(parts, 0, dim)
    lengths = parts.shape
    return parts.reshape(*lengths[:dim], lengths[dim] * lengths[dim + 1], *lengths[dim + 2 :])


def turned_blocks(parts, axes, sequence):
    lengths = [lax.axis_size(a) for a in axes]
    parts = parts.reshape(*lengths, *parts.shape[1:])
    for k in sequence:
        parts = lax.all_to_all(parts, axes[k], split_axis=k, concat_axis=k, tiled=True)
    return parts.reshape(-1, *parts.shape[len(axes) :])


def core_and_chips(x, groups, sequence, split_dim, concat_dim):
    count = lax.axis_size(groups[0]) * lax.axis_size(groups[1])
    parts = split_up(x, split_dim, count)
    return laid_out(turned_blocks(parts, groups, sequence), concat_dim)


def copy_for_each(x, axis):
    copies = jnp.broadcast_to(x, (lax.axis_size(axis), *x.shape))
    return lax.all_to_all(copies, axis, split_axis=0, concat_axis=0, tiled=True)


def collected_together(x, axis):
    leaves = jax.tree.leaves(x)
    sequence = sorted(range(len(leaves)), key=lambda k: -leaves[k].size)
    width = (1, *leaves[sequence[0]].shape)[-1]
    lines = [
        jnp.pad(leaves[k].reshape(-1), (0, -leaves[k].size % width)).reshape(-1, width)
        for k in sequence
    ]
    both, at, found = (copy_for_each(jnp.concatenate(lines), axis), 0, {})
    for k, line in zip(sequence, lines):
        piece = both[:, at : at + len(line)].reshape(len(both), -1)
        found[k] = piece[:, : leaves[k].size].reshape(-1, *leaves[k].shape)
        at += len(line)
    numbers = iter(range(len(leaves)))
    return jax.tree.map(lambda _: found[next(numbers)], x)


def combined_pairwise(pieces, combine):
    while len(jax.tree.leaves(pieces)[0]) > 1:
        pieces = jax.vmap(combine)(
            *(jax.tree.map(lambda part: part[side::2], pieces) for side in (0, 1))
        )
    return jax.tree.map(lambda part: part[0], pieces)


def carried_in(x, axis, combine, identity):
    count, index = (lax.axis_size(axis), lax.axis_index(axis))
    passed = jnp.arange(count) < index

    def kept(part, zero, own):
        part = jnp.where(
            passed.reshape(-1, *(1 for _ in own.shape)), part, jnp.asarray(zero, own.dtype)
        )
        return part

    pieces = collected_together(x, axis)
    return combined_pairwise(jax.tree.map(kept, pieces, identity, x), combine)


def basis_coefficients(nodes, chosen):
    polynomial = [1.0]
    for other, point in enumerate(nodes):
        if other == chosen:
            continue
        divisor = nodes[chosen] - point
        widened = [0.0] * (len(polynomial) + 1)
        for power, value in enumerate(polynomial):
            widened[power + 1] += value / divisor
            widened[power] -= value * point / divisor
        polynomial = widened
    return polynomial


def basis_value(nodes, chosen, where):
    result = 1.0
    for other, point in enumerate(nodes):
        if other != chosen:
            result *= (where - point) / (nodes[chosen] - point)
    return result


def node_tables():
    root = math.sqrt(3.0 / 7.0)
    fine_tau = [0.0, (1.0 - root) / 2.0, 0.5, (1.0 + root) / 2.0, 1.0]
    coarse_tau = [0.0, 0.5, 1.0]
    integ = []
    for j in range(4):
        row_values = []
        for k in range(5):
            polynomial = basis_coefficients(fine_tau, k)
            total = 0.0
            for power, value in enumerate(polynomial):
                total += (
                    value
                    * (fine_tau[j + 1] ** (power + 1) - fine_tau[j] ** (power + 1))
                    / (power + 1)
                )
            row_values.append(total)
        integ.append(row_values)
    interp = [[basis_value(coarse_tau, c, fine_tau[m]) for c in range(3)] for m in range(5)]
    spacing = [float(fine_tau[j + 1] - fine_tau[j]) for j in range(4)]
    return (jnp.asarray(integ, jnp.float32), spacing, jnp.asarray(interp, jnp.float32))


def hartley(length):
    counter = jnp.arange(length, dtype=jnp.int32)
    product = counter[:, None] * counter[None, :] % length
    phase = 2.0 * jnp.pi * product.astype(jnp.float32) / length
    return (jnp.cos(phase) + jnp.sin(phase)) / math.sqrt(length)


def local_force(padded):
    field = padded[:, 1:-1]
    near = padded[:, 2:] + padded[:, :-2] + jnp.roll(field, 1, 2) + jnp.roll(field, -1, 2)
    near = near + jnp.roll(field, 1, 3) + jnp.roll(field, -1, 3)
    return diffusion * (near - 6.0 * field) + reaction * (field - field * field * field)


def inner_planes(field, margin):
    return field[margin : field.shape[0] - margin]


def restrict(field):
    depth, rows, cols = field.shape
    return (
        field.reshape(depth // 2, 2, rows // 2, 2, cols // 2, 2)
        .mean(axis=(1, 3, 5))
        .reshape(depth // 2, rows * cols // 4)
    )


def compose(earlier, later):
    return (later[0] * earlier[0], later[0] * earlier[1] + later[1])


def shards(u_old, u_init):
    integ, spacing, interp = node_tables()
    highest = lax.Precision.HIGHEST
    depth, rows, cols = u_init.shape
    fine_old = u_old[0]
    previous = passed_along(fine_old[4], "tm", 1)
    position = lax.axis_index("tm")
    start = jnp.where(position == 0, u_init, previous)
    states = [start]
    forces = []
    together = jnp.concatenate([start[None], fine_old], 0)
    wide = padded_2(together, ((SPACE, 1),), 5)
    fold_wide = local_force(wide[1:])
    iold_wide = step_length * jnp.einsum("jk,kzxy->jzxy", integ, fold_wide, precision=highest)
    current = wide[0]
    for section in range(4):
        force_now = local_force(current[None])[0]
        forces.append(inner_planes(force_now, 4 - section))
        following = (
            inner_planes(current, 1)
            + step_length
            * spacing[section]
            * (force_now - inner_planes(fold_wide[section], section))
            + inner_planes(iold_wide[section], section)
        )
        states.append(inner_planes(following, 4 - section))
        current = following
    forces.append(local_force(current[None])[0])
    inew = step_length * jnp.einsum("jk,kzxy->jzxy", integ, jnp.stack(forces), precision=highest)
    stacked = jnp.stack(
        [
            restrict(states[0]),
            restrict(states[2]),
            restrict(states[4]),
            restrict(inew[0] + inew[1]),
            restrict(inew[2] + inew[3]),
            restrict(u_init),
        ]
    )
    planes_c = depth // 2
    rows_c = rows // 2
    cols_c = cols // 2
    depth_c = planes_c * lax.axis_size(SPACE)
    table_xy = jnp.kron(hartley(rows_c), hartley(cols_c))
    table_z = hartley(depth_c)
    spectral_xy = jnp.einsum("fzc,cd->fzd", stacked, table_xy, precision=highest)
    wave_z = jnp.arange(depth_c, dtype=jnp.int32)
    wave_xy = jnp.arange(rows_c * cols_c, dtype=jnp.int32)
    angle_z = 2.0 * jnp.cos(2.0 * jnp.pi * wave_z.astype(jnp.float32) / depth_c)
    angle_x = 2.0 * jnp.cos(2.0 * jnp.pi * (wave_xy // cols_c).astype(jnp.float32) / rows_c)
    angle_y = 2.0 * jnp.cos(2.0 * jnp.pi * (wave_xy % cols_c).astype(jnp.float32) / cols_c)
    eigen_all = 0.25 * (angle_z[:, None] + angle_x[None, :] + angle_y[None, :] - 6.0)
    place = lax.axis_index(SPACE)
    columns = core_and_chips(spectral_xy, (("space_0", "space_1"), "space_2"), (1, 0), 2, 1)
    spectra = jnp.einsum("qz,fzc->fqc", table_z, columns, precision=highest)
    width = columns.shape[2]
    eigen = lax.dynamic_slice_in_dim(eigen_all, place * width, width, 1)
    pieces = [spectra[k] for k in range(6)]
    damping = 0.5 * step_length * diffusion * eigen
    denom = 1.0 - damping
    lifted0 = pieces[3] - damping * pieces[1]
    lifted1 = pieces[4] - damping * pieces[2]
    slope = 1.0 / (denom * denom)
    offset = (lifted0 / denom + lifted1) / denom
    before_slope, before_offset = carried_in(
        (slope, offset), "tm", compose, (jnp.ones_like(slope), jnp.zeros_like(offset))
    )
    begin = before_slope * pieces[5] + before_offset
    middle = (begin + lifted0) / denom
    finish = (middle + lifted1) / denom
    delta = jnp.stack([begin - pieces[0], middle - pieces[1], finish - pieces[2]])
    planar = jnp.einsum("zq,fqc->fzc", table_z, delta, precision=highest)
    returned = lax.all_to_all(planar, SPACE, split_axis=1, concat_axis=2, tiled=True)
    real_space = jnp.einsum("fzc,cd->fzd", returned, table_xy, precision=highest)
    coarse_grid = real_space.reshape(3, planes_c, rows_c, cols_c)
    timed = jnp.einsum("mc,czxy->mzxy", interp, coarse_grid, precision=highest)
    upper = jnp.repeat(jnp.repeat(jnp.repeat(timed, 2, 1), 2, 2), 2, 3)
    return (jnp.stack(states) + upper)[None]


def solution(mesh):
    finer = Mesh(
        mesh.devices.reshape(mesh.shape["tm"], 4, 2, 2), ("tm", "space_0", "space_1", "space_2")
    )
    in_specs = (P("tm", None, SPACE, None, None), P(SPACE, None, None))
    out_specs = P("tm", None, SPACE, None, None)
    return jax.shard_map(
        shards, mesh=finer, in_specs=in_specs, out_specs=out_specs, check_vma=False
    )
```

profile of v0, /device:TPU:1, one launch (start us, length us, event | category | flops | bytes accessed | tf_op | source)
XLA Modules:
  0.0 267.7 jit_solution(8408288563641661195)
XLA Ops:
  0.0 0.9 slice_bitcast_fusion.2
  0.9 4.4 %collective-permute-start = (f32[16,16,128]{2,1,0:T(8,128)S(1)}, f32[16,16,128]{2,1,0:T(8,128)S(1)}, u32[]{:S(2)}, u32[]{:S(2)}) collective-permute-start(f32[16,16,128]{2,1,0:T(8,128)S(1)} %slice_bitcast_fusion.2), channel_id=1, source_target_pairs={{0,16},{16,32},{32,48},{48,64},{64,80},{80,96},{96,112},{112,128},... | collective-permute-start | bytes 393224 | tf_op jit(solution)/shard_map/ppermute | solution.py:17
  5.5 10.5 %reshape.343 = f32[8,2,8,2,64,2]{5,4,3,2,1,0:T(8,128)} reshape(f32[16,16,128]{2,1,0:T(8,128)} %param.5) | data formatting | bytes 262144 | tf_op jit(solution)/shard_map/reshape | solution.py:168
  16.0 4.0 %reduce_sum.59 = f32[8,8,64]{2,1,0:T(8,128)S(1)} reduce(f32[8,2,8,2,64,2]{5,4,3,2,1,0:T(8,128)} %reshape.343, f32[]{:T(128)} %constant.162.clone.1), dimensions={1,3,5}, to_apply=%region_5.6 | reduce | flops 28672 | bytes 147460 | tf_op jit(solution)/shard_map/reduce_sum | solution.py:169
  20.0 1.5 broadcast_multiply_fusion
  21.7 2.0 mul.366
  23.7 0.7 bitcast_dynamic-update-slice_fusion.2
  24.3 9.7 %reshape.340 = f32[8,2,8,2,64,2]{5,4,3,2,1,0:T(8,128)} reshape(f32[16,16,128]{2,1,0:T(8,128)S(1)} %get-tuple-element.20) | data formatting | bytes 262144 | tf_op jit(solution)/shard_map/reshape | solution.py:168
  34.1 15.4 %collective-permute-start.1 = (f32[6,5,16,128]{3,2,1,0:T(8,128)S(1)}, f32[6,5,16,128]{3,2,1,0:T(8,128)S(1)}, u32[]{:S(2)}, u32[]{:S(2)}) collective-permute-start(f32[6,5,16,128]{3,2,1,0:T(8,128)S(1)} %get-tuple-element.35), channel_id=1, source_target_pairs={{0,1},{1,2},{2,3},{3,4},{4,5},{5,6},{6,7},{7,8},{8,9},{9,10},{10,1... | collective-permute-start | bytes 737288 | tf_op jit(solution)/shard_map/ppermute | solution.py:27
  49.5 2.1 collective-permute-start.2
  51.6 4.0 %reduce_sum.54 = f32[8,8,64]{2,1,0:T(8,128)S(1)} reduce(f32[8,2,8,2,64,2]{5,4,3,2,1,0:T(8,128)} %reshape.340, f32[]{:T(128)} %constant.162.clone.1), dimensions={1,3,5}, to_apply=%region_0.1 | reduce | flops 28672 | bytes 147460 | tf_op jit(solution)/shard_map/reduce_sum | solution.py:169
  55.7 13.5 %collective-permute-done.1 = f32[6,5,16,128]{3,2,1,0:T(8,128)S(1)} collective-permute-done((f32[6,5,16,128]{3,2,1,0:T(8,128)S(1)}, f32[6,5,16,128]{3,2,1,0:T(8,128)S(1)}, u32[]{:S(2)}, u32[]{:S(2)}) %collective-permute-start.1) | collective-permute-done | bytes 245792 | tf_op jit(solution)/shard_map/ppermute | solution.py:27
  69.2 7.4 %collective-permute-done.2 = f32[6,5,16,128]{3,2,1,0:T(8,128)S(1)} collective-permute-done((f32[6,5,16,128]{3,2,1,0:T(8,128)S(1)}, f32[6,5,16,128]{3,2,1,0:T(8,128)S(1)}, u32[]{:S(2)}, u32[]{:S(2)}) %collective-permute-start.2) | collective-permute-done | bytes 245792 | tf_op jit(solution)/shard_map/ppermute | solution.py:28
  77.8 0.9 fusion.4
  78.7 2.0 fusion
  82.9 1.4 fusion.2
  84.3 0.8 fusion.51
  85.1 10.0 %add.346 = f32[8,2,8,2,64,2]{5,4,3,2,1,0:T(8,128)} reshape(f32[16,16,128]{2,1,0:T(8,128)S(1)} %get-tuple-element.6) | data formatting | bytes 262144 | tf_op jit(solution)/shard_map/add | solution.py:212
  95.1 4.0 %reduce_sum.57 = f32[8,8,64]{2,1,0:T(8,128)S(1)} reduce(f32[8,2,8,2,64,2]{5,4,3,2,1,0:T(8,128)} %add.346, f32[]{:T(128)} %constant.162.clone.1), dimensions={1,3,5}, to_apply=%region_3.4 | reduce | flops 28672 | bytes 147460 | tf_op jit(solution)/shard_map/reduce_sum | solution.py:169
  99.2 9.7 %reshape.342 = f32[8,2,8,2,64,2]{5,4,3,2,1,0:T(8,128)} reshape(f32[1,16,16,128]{3,2,1,0:T(8,128)S(1)} %get-tuple-element.66) | data formatting | bytes 262144 | tf_op jit(solution)/shard_map/reshape | solution.py:168
  109.0 4.0 %reduce_sum.56 = f32[8,8,64]{2,1,0:T(8,128)S(1)} reduce(f32[8,2,8,2,64,2]{5,4,3,2,1,0:T(8,128)} %reshape.342, f32[]{:T(128)} %constant.162.clone.1), dimensions={1,3,5}, to_apply=%region_2.3 | reduce | flops 28672 | bytes 147460 | tf_op jit(solution)/shard_map/reduce_sum | solution.py:169
  113.1 9.7 %reshape.341 = f32[8,2,8,2,64,2]{5,4,3,2,1,0:T(8,128)} reshape(f32[1,16,16,128]{3,2,1,0:T(8,128)S(1)} %slice.664) | data formatting | bytes 262144 | tf_op jit(solution)/shard_map/reshape | solution.py:168
  122.8 4.0 %reduce_sum.55 = f32[8,8,64]{2,1,0:T(8,128)S(1)} reduce(f32[8,2,8,2,64,2]{5,4,3,2,1,0:T(8,128)} %reshape.341, f32[]{:T(128)} %constant.162.clone.1), dimensions={1,3,5}, to_apply=%region_1.2 | reduce | flops 28672 | bytes 147460 | tf_op jit(solution)/shard_map/reduce_sum | solution.py:169
  126.9 9.7 %add.348 = f32[8,2,8,2,64,2]{5,4,3,2,1,0:T(8,128)} reshape(f32[16,16,128]{2,1,0:T(8,128)S(1)} %get-tuple-element.5) | data formatting | bytes 262144 | tf_op jit(solution)/shard_map/add | solution.py:213
  136.6 4.0 %reduce_sum.58 = f32[8,8,64]{2,1,0:T(8,128)S(1)} reduce(f32[8,2,8,2,64,2]{5,4,3,2,1,0:T(8,128)} %add.348, f32[]{:T(128)} %constant.162.clone.1), dimensions={1,3,5}, to_apply=%region_4.5 | reduce | flops 28672 | bytes 147460 | tf_op jit(solution)/shard_map/reduce_sum | solution.py:169
  140.8 2.6 fusion.62
  143.6 3.5 %all_to_all.33 = f32[2,1,12288]{2,1,0:T(1,128)S(1)} all-to-all(f32[2,1,12288]{2,1,0:T(1,128)S(1)} %reshape.389), channel_id=1, replica_groups=mesh['tm'=32,'space_0'=4,'space_1'=2,'space_2'=2] {'space_2'}, dimensions={0} | all-to-all | bytes 196608 | tf_op jit(solution)/shard_map/all_to_all | solution.py:48
  147.6 0.9 reduce.8
  148.8 0.8 reshape.391
  149.6 8.5 %all-to-all-start.1 = ((f32[8,1,3072]{2,1,0:T(1,128)}), f32[8,1,3072]{2,1,0:T(1,128)S(1)}, u32[]{:S(2)}, u32[]{:S(2)}) async-start(f32[8,1,3072]{2,1,0:T(1,128)} %reshape.391), calls=%async_computation.1 | async-start | bytes 196608 | tf_op jit(solution)/shard_map/all_to_all | solution.py:48
  158.4 13.8 %all-to-all-done.1 = f32[8,1,3072]{2,1,0:T(1,128)S(1)} async-done(((f32[8,1,3072]{2,1,0:T(1,128)}), f32[8,1,3072]{2,1,0:T(1,128)S(1)}, u32[]{:S(2)}, u32[]{:S(2)}) %all-to-all-start.1) | async-done | bytes 98336 | tf_op jit(solution)/shard_map/all_to_all | solution.py:48
  172.2 0.9 reduce.9
  173.2 0.8 convolution_bitcast_fusion
  174.2 1.1 broadcast_in_dim.60
  175.3 7.4 %all-to-all-start.2 = ((f32[32,256,32]{1,2,0:T(8,128)}), f32[32,256,32]{1,2,0:T(8,128)S(1)}, u32[]{:S(2)}, u32[]{:S(2)}) async-start(f32[32,256,32]{1,2,0:T(8,128)} %broadcast_in_dim.60), calls=%async_computation.2 | async-start | bytes 2097152 | tf_op jit(solution)/shard_map/all_to_all | solution.py:60
  182.7 0.7 fusion.59
  183.4 0.7 bitcast_dynamic-update-slice_fusion.1
  184.1 0.7 fusion.58
  184.7 48.1 %all-to-all-done.2 = f32[32,256,32]{1,2,0:T(8,128)S(1)} async-done(((f32[32,256,32]{1,2,0:T(8,128)}), f32[32,256,32]{1,2,0:T(8,128)S(1)}, u32[]{:S(2)}, u32[]{:S(2)}) %all-to-all-start.2) | async-done | bytes 1048608 | tf_op jit(solution)/shard_map/all_to_all | solution.py:60
  234.0 0.8 reshape.393
  234.8 7.0 %all-to-all-start.3 = ((f32[16,1,768]{2,1,0:T(1,128)}), f32[16,1,768]{2,1,0:T(1,128)S(1)}, u32[]{:S(2)}, u32[]{:S(2)}) async-start(f32[16,1,768]{2,1,0:T(1,128)} %reshape.393), calls=%async_computation.3 | async-start | bytes 98304 | tf_op jit(solution)/shard_map/all_to_all | solution.py:250
  242.6 13.9 %all-to-all-done.3 = f32[16,1,768]{2,1,0:T(1,128)S(1)} async-done(((f32[16,1,768]{2,1,0:T(1,128)}), f32[16,1,768]{2,1,0:T(1,128)S(1)}, u32[]{:S(2)}, u32[]{:S(2)}) %all-to-all-start.3) | async-done | bytes 49184 | tf_op jit(solution)/shard_map/all_to_all | solution.py:250
  256.4 0.7 reduce.10
  257.6 1.4 fusion.77
  259.7 1.1 copy.109
  260.7 2.8 %broadcast_in_dim.65 = f32[5,16,16,64,2]{2,1,4,3,0:T(8,128)} broadcast(f32[5,16,16,64]{2,1,3,0:T(8,128)S(1)} %copy.109), dimensions={0,1,2,3} | broadcast | bytes 983040 | tf_op jit(solution)/shard_map/broadcast_in_dim | solution.py:254
  263.5 3.3 %copy.110 = f32[1,5,16,16,128]{4,3,2,1,0:T(8,128)S(1)} copy(f32[1,5,16,16,128]{3,2,4,1,0:T(8,128)} %bitcast.144) | data formatting | bytes 1310720 | tf_op jit(solution)/shard_map/reshape | solution.py:254
  266.8 0.9 add.365
  (100 shorter events, 8.4 us)
Async XLA Ops:
  0.9 22.7 %collective-permute-start = (f32[16,16,128]{2,1,0:T(8,128)S(1)}, f32[16,16,128]{2,1,0:T(8,128)S(1)}, u32[]{:S(2)}, u32[]{:S(2)}) collective-permute-start(f32[16,16,128]{2,1,0:T(8,128)S(1)} %slice_bitcast_fusion.2), channel_id=1, source_target_pairs={{0,16},{16,32},{32,48},{48,64},{64,80},{80,96},{96,112},{112,128},... | collective-permute-start | bytes 393224 | tf_op jit(solution)/shard_map/ppermute | solution.py:17
  21.7 2.0 copy-start.2
  24.3 9.7 %copy-start = (f32[1,5,16,16,128]{4,3,2,1,0:T(8,128)S(1)}, f32[1,5,16,16,128]{4,3,2,1,0:T(8,128)}, u32[]{:S(2)}) copy-start(f32[1,5,16,16,128]{4,3,2,1,0:T(8,128)} %param.4) | copy-start | bytes 1966084
  34.1 35.1 %collective-permute-start.1 = (f32[6,5,16,128]{3,2,1,0:T(8,128)S(1)}, f32[6,5,16,128]{3,2,1,0:T(8,128)S(1)}, u32[]{:S(2)}, u32[]{:S(2)}) collective-permute-start(f32[6,5,16,128]{3,2,1,0:T(8,128)S(1)} %get-tuple-element.35), channel_id=1, source_target_pairs={{0,1},{1,2},{2,3},{3,4},{4,5},{5,6},{6,7},{7,8},{8,9},{9,10},{10,1... | collective-permute-start | bytes 737288 | tf_op jit(solution)/shard_map/ppermute | solution.py:27
  49.5 27.1 %collective-permute-start.2 = (f32[6,5,16,128]{3,2,1,0:T(8,128)S(1)}, f32[6,5,16,128]{3,2,1,0:T(8,128)S(1)}, u32[]{:S(2)}, u32[]{:S(2)}) collective-permute-start(f32[6,5,16,128]{3,2,1,0:T(8,128)S(1)} %get-tuple-element.36), channel_id=1, source_target_pairs={{1,0},{2,1},{3,2},{4,3},{5,4},{6,5},{7,6},{8,7},{9,8},{10,9},{11,1... | collective-permute-start | bytes 737288 | tf_op jit(solution)/shard_map/ppermute | solution.py:28
  77.8 0.9 copy-start.3
  149.6 22.6 %all-to-all-start.1 = ((f32[8,1,3072]{2,1,0:T(1,128)}), f32[8,1,3072]{2,1,0:T(1,128)S(1)}, u32[]{:S(2)}, u32[]{:S(2)}) async-start(f32[8,1,3072]{2,1,0:T(1,128)} %reshape.391), calls=%async_computation.1 | async-start | bytes 196608 | tf_op jit(solution)/shard_map/all_to_all | solution.py:48
  175.3 57.5 %all-to-all-start.2 = ((f32[32,256,32]{1,2,0:T(8,128)}), f32[32,256,32]{1,2,0:T(8,128)S(1)}, u32[]{:S(2)}, u32[]{:S(2)}) async-start(f32[32,256,32]{1,2,0:T(8,128)} %broadcast_in_dim.60), calls=%async_computation.2 | async-start | bytes 2097152 | tf_op jit(solution)/shard_map/all_to_all | solution.py:60
  234.8 21.6 %all-to-all-start.3 = ((f32[16,1,768]{2,1,0:T(1,128)}), f32[16,1,768]{2,1,0:T(1,128)S(1)}, u32[]{:S(2)}, u32[]{:S(2)}) async-start(f32[16,1,768]{2,1,0:T(1,128)} %reshape.393), calls=%async_computation.3 | async-start | bytes 98304 | tf_op jit(solution)/shard_map/all_to_all | solution.py:250
  257.2 1.8 copy-start.4
  263.5 3.3 %copy-start.1 = (f32[1,5,16,16,128]{4,3,2,1,0:T(8,128)S(1)}, f32[1,5,16,16,128]{4,3,2,1,0:T(8,128)}, u32[]{:S(2)}) copy-start(f32[1,5,16,16,128]{4,3,2,1,0:T(8,128)} %bitcast_dynamic-update-slice_fusion) | copy-start | bytes 1966084
where the time goes:
time: 269 us; the launch traced here: 268 us
  waiting for transfers between devices  96.6 us (36%)
  local copies, waits for them, and re-layouts  79.5 us (30%)
  starting transfers between devices  44.8 us (17%)
  other arithmetic  33.6 us (12%)
  matrix products  9.05 us (3%)
  blocking collectives  3.45 us (1%)
    all_to_all x1, waiting for transfers between devices, copy_for_each(): return lax.all_to_all(copies, axis, split_axis=0, concat_axis=0, tiled=True)  48.1 us
    reshape x4, local copies, waits for them, and re-layouts, restrict(): field.reshape(depth // 2, 2, rows // 2, 2, cols // 2, 2)  39.7 us
    reduce_sum x6, other arithmetic, restrict(): return field.reshape(depth // 2, 2, rows // 2, 2, cols // 2, 2).mean(axis...  24.1 us
    ppermute x1, starting transfers between devices, padded_2(): before = lax.ppermute(last, axis, up)  15.4 us
    all_to_all x1, waiting for transfers between devices, shards(): lax.all_to_all(planar, SPACE, split_axis=1, concat_axis=2, tiled=True)  13.9 us
    all_to_all x1, waiting for transfers between devices, turned_blocks(): lax.all_to_all(parts, axes[k], split_axis=k, concat_axis=k, tiled=True)  13.8 us
    ppermute x1, waiting for transfers between devices, padded_2(): before = lax.ppermute(last, axis, up)  13.5 us
    add x1, local copies, waits for them, and re-layouts, shards(): inew[0] + inew[1]  9.98 us
  transfers between devices with their start and end apart: 6, of which 5 were waited for; matrix products, arithmetic and copies ran while one was open for 9% of the time, Pallas kernels for 0%

commit v1 on v0

--- a/solution.py
+++ b/solution.py
@@ -247,7 +247,10 @@
     finish = (middle + lifted1) / denom
     delta = jnp.stack([begin - pieces[0], middle - pieces[1], finish - pieces[2]])
     planar = jnp.einsum("zq,fqc->fzc", table_z, delta, precision=highest)
-    returned = lax.all_to_all(planar, SPACE, split_axis=1, concat_axis=2, tiled=True)
+    returned = jnp.concatenate(
+        lax.all_to_all(jnp.stack(jnp.split(planar, lax.axis_size(SPACE), axis=1)), SPACE, 0, 0),
+        axis=2,
+    )
     real_space = jnp.einsum("fzc,cd->fzd", returned, table_xy, precision=highest)
     coarse_grid = real_space.reshape(3, planes_c, rows_c, cols_c)
     timed = jnp.einsum("mc,czxy->mzxy", interp, coarse_grid, precision=highest)

time: 269 us -> 270 us (level)
  no operation moved by 1% of the time
where the time goes in v1:
time: 270 us; the launch traced here: 269 us
  waiting for transfers between devices  96.6 us (36%)
  local copies, waits for them, and re-layouts  80.8 us (30%)
  starting transfers between devices  44.9 us (17%)
  other arithmetic  33.6 us (12%)
  matrix products  9.05 us (3%)
  blocking collectives  3.45 us (1%)
    all_to_all x1, waiting for transfers between devices, copy_for_each(): return lax.all_to_all(copies, axis, split_axis=0, concat_axis=0, tiled=True)  48.1 us
    reshape x4, local copies, waits for them, and re-layouts, restrict(): field.reshape(depth // 2, 2, rows // 2, 2, cols // 2, 2)  39.7 us
    reduce_sum x6, other arithmetic, restrict(): return field.reshape(depth // 2, 2, rows // 2, 2, cols // 2, 2).mean(axis...  24.1 us
    ppermute x1, starting transfers between devices, padded_2(): before = lax.ppermute(last, axis, up)  15.4 us
    all_to_all x1, waiting for transfers between devices, shards(): lax.all_to_all(jnp.stack(jnp.split(planar, lax.axis_size(SPACE), axis=1))...  13.9 us
    all_to_all x1, waiting for transfers between devices, turned_blocks(): lax.all_to_all(parts, axes[k], split_axis=k, concat_axis=k, tiled=True)  13.8 us
    ppermute x1, waiting for transfers between devices, padded_2(): before = lax.ppermute(last, axis, up)  13.5 us
    add x1, local copies, waits for them, and re-layouts, shards(): inew[0] + inew[1]  9.97 us
  transfers between devices with their start and end apart: 6, of which 5 were waited for; matrix products, arithmetic and copies ran while one was open for 9% of the time, Pallas kernels for 0%

profile of v1, /device:TPU:1, one launch (start us, length us, event | category | flops | bytes accessed | tf_op | source)
XLA Modules:
  0.0 269.2 jit_solution(9572170724353152795)
XLA Ops:
  0.0 0.9 slice_bitcast_fusion.2
  0.9 4.4 %collective-permute-start = (f32[16,16,128]{2,1,0:T(8,128)S(1)}, f32[16,16,128]{2,1,0:T(8,128)S(1)}, u32[]{:S(2)}, u32[]{:S(2)}) collective-permute-start(f32[16,16,128]{2,1,0:T(8,128)S(1)} %slice_bitcast_fusion.2), channel_id=1, source_target_pairs={{0,16},{16,32},{32,48},{48,64},{64,80},{80,96},{96,112},{112,128},... | collective-permute-start | bytes 393224 | tf_op jit(solution)/shard_map/ppermute | solution.py:17
  5.5 10.5 %reshape.349 = f32[8,2,8,2,64,2]{5,4,3,2,1,0:T(8,128)} reshape(f32[16,16,128]{2,1,0:T(8,128)} %param.5) | data formatting | bytes 262144 | tf_op jit(solution)/shard_map/reshape | solution.py:168
  16.0 4.0 %reduce_sum.59 = f32[8,8,64]{2,1,0:T(8,128)S(1)} reduce(f32[8,2,8,2,64,2]{5,4,3,2,1,0:T(8,128)} %reshape.349, f32[]{:T(128)} %constant.162.clone.1), dimensions={1,3,5}, to_apply=%region_5.6 | reduce | flops 28672 | bytes 147460 | tf_op jit(solution)/shard_map/reduce_sum | solution.py:169
  20.0 1.5 broadcast_multiply_fusion
  21.7 2.0 mul.366
  23.7 0.7 bitcast_dynamic-update-slice_fusion.2
  24.3 9.7 %reshape.346 = f32[8,2,8,2,64,2]{5,4,3,2,1,0:T(8,128)} reshape(f32[16,16,128]{2,1,0:T(8,128)S(1)} %get-tuple-element.20) | data formatting | bytes 262144 | tf_op jit(solution)/shard_map/reshape | solution.py:168
  34.1 15.4 %collective-permute-start.1 = (f32[6,5,16,128]{3,2,1,0:T(8,128)S(1)}, f32[6,5,16,128]{3,2,1,0:T(8,128)S(1)}, u32[]{:S(2)}, u32[]{:S(2)}) collective-permute-start(f32[6,5,16,128]{3,2,1,0:T(8,128)S(1)} %get-tuple-element.35), channel_id=1, source_target_pairs={{0,1},{1,2},{2,3},{3,4},{4,5},{5,6},{6,7},{7,8},{8,9},{9,10},{10,1... | collective-permute-start | bytes 737288 | tf_op jit(solution)/shard_map/ppermute | solution.py:27
  49.5 2.1 collective-permute-start.2
  51.6 4.0 %reduce_sum.54 = f32[8,8,64]{2,1,0:T(8,128)S(1)} reduce(f32[8,2,8,2,64,2]{5,4,3,2,1,0:T(8,128)} %reshape.346, f32[]{:T(128)} %constant.162.clone.1), dimensions={1,3,5}, to_apply=%region_0.1 | reduce | flops 28672 | bytes 147460 | tf_op jit(solution)/shard_map/reduce_sum | solution.py:169
  55.7 13.5 %collective-permute-done.1 = f32[6,5,16,128]{3,2,1,0:T(8,128)S(1)} collective-permute-done((f32[6,5,16,128]{3,2,1,0:T(8,128)S(1)}, f32[6,5,16,128]{3,2,1,0:T(8,128)S(1)}, u32[]{:S(2)}, u32[]{:S(2)}) %collective-permute-start.1) | collective-permute-done | bytes 245792 | tf_op jit(solution)/shard_map/ppermute | solution.py:27
  69.2 7.4 %collective-permute-done.2 = f32[6,5,16,128]{3,2,1,0:T(8,128)S(1)} collective-permute-done((f32[6,5,16,128]{3,2,1,0:T(8,128)S(1)}, f32[6,5,16,128]{3,2,1,0:T(8,128)S(1)}, u32[]{:S(2)}, u32[]{:S(2)}) %collective-permute-start.2) | collective-permute-done | bytes 245792 | tf_op jit(solution)/shard_map/ppermute | solution.py:28
  77.8 0.9 fusion.4
  78.7 2.0 fusion
  82.9 1.4 fusion.2
  84.3 0.8 fusion.51
  85.1 10.0 %add.346 = f32[8,2,8,2,64,2]{5,4,3,2,1,0:T(8,128)} reshape(f32[16,16,128]{2,1,0:T(8,128)S(1)} %get-tuple-element.6) | data formatting | bytes 262144 | tf_op jit(solution)/shard_map/add | solution.py:212
  95.1 4.0 %reduce_sum.57 = f32[8,8,64]{2,1,0:T(8,128)S(1)} reduce(f32[8,2,8,2,64,2]{5,4,3,2,1,0:T(8,128)} %add.346, f32[]{:T(128)} %constant.162.clone.1), dimensions={1,3,5}, to_apply=%region_3.4 | reduce | flops 28672 | bytes 147460 | tf_op jit(solution)/shard_map/reduce_sum | solution.py:169
  99.2 9.7 %reshape.348 = f32[8,2,8,2,64,2]{5,4,3,2,1,0:T(8,128)} reshape(f32[1,16,16,128]{3,2,1,0:T(8,128)S(1)} %get-tuple-element.66) | data formatting | bytes 262144 | tf_op jit(solution)/shard_map/reshape | solution.py:168
  108.9 4.0 %reduce_sum.56 = f32[8,8,64]{2,1,0:T(8,128)S(1)} reduce(f32[8,2,8,2,64,2]{5,4,3,2,1,0:T(8,128)} %reshape.348, f32[]{:T(128)} %constant.162.clone.1), dimensions={1,3,5}, to_apply=%region_2.3 | reduce | flops 28672 | bytes 147460 | tf_op jit(solution)/shard_map/reduce_sum | solution.py:169
  113.0 9.7 %reshape.347 = f32[8,2,8,2,64,2]{5,4,3,2,1,0:T(8,128)} reshape(f32[1,16,16,128]{3,2,1,0:T(8,128)S(1)} %slice.664) | data formatting | bytes 262144 | tf_op jit(solution)/shard_map/reshape | solution.py:168
  122.8 4.0 %reduce_sum.55 = f32[8,8,64]{2,1,0:T(8,128)S(1)} reduce(f32[8,2,8,2,64,2]{5,4,3,2,1,0:T(8,128)} %reshape.347, f32[]{:T(128)} %constant.162.clone.1), dimensions={1,3,5}, to_apply=%region_1.2 | reduce | flops 28672 | bytes 147460 | tf_op jit(solution)/shard_map/reduce_sum | solution.py:169
  126.9 9.7 %add.348 = f32[8,2,8,2,64,2]{5,4,3,2,1,0:T(8,128)} reshape(f32[16,16,128]{2,1,0:T(8,128)S(1)} %get-tuple-element.5) | data formatting | bytes 262144 | tf_op jit(solution)/shard_map/add | solution.py:213
  136.6 4.0 %reduce_sum.58 = f32[8,8,64]{2,1,0:T(8,128)S(1)} reduce(f32[8,2,8,2,64,2]{5,4,3,2,1,0:T(8,128)} %add.348, f32[]{:T(128)} %constant.162.clone.1), dimensions={1,3,5}, to_apply=%region_4.5 | reduce | flops 28672 | bytes 147460 | tf_op jit(solution)/shard_map/reduce_sum | solution.py:169
  140.7 2.6 fusion.62
  143.6 3.5 %all_to_all.20 = f32[2,1,12288]{2,1,0:T(1,128)S(1)} all-to-all(f32[2,1,12288]{2,1,0:T(1,128)S(1)} %reshape.397), channel_id=1, replica_groups=mesh['tm'=32,'space_0'=4,'space_1'=2,'space_2'=2] {'space_2'}, dimensions={0} | all-to-all | bytes 196608 | tf_op jit(solution)/shard_map/all_to_all | solution.py:48
  147.6 0.9 reduce.8
  148.8 0.9 reshape.399
  149.6 8.5 %all-to-all-start.1 = ((f32[8,1,3072]{2,1,0:T(1,128)}), f32[8,1,3072]{2,1,0:T(1,128)S(1)}, u32[]{:S(2)}, u32[]{:S(2)}) async-start(f32[8,1,3072]{2,1,0:T(1,128)} %reshape.399), calls=%async_computation.1 | async-start | bytes 196608 | tf_op jit(solution)/shard_map/all_to_all | solution.py:48
  158.4 13.8 %all-to-all-done.1 = f32[8,1,3072]{2,1,0:T(1,128)S(1)} async-done(((f32[8,1,3072]{2,1,0:T(1,128)}), f32[8,1,3072]{2,1,0:T(1,128)S(1)}, u32[]{:S(2)}, u32[]{:S(2)}) %all-to-all-start.1) | async-done | bytes 98336 | tf_op jit(solution)/shard_map/all_to_all | solution.py:48
  172.2 0.9 reduce.9
  173.3 0.8 convolution_bitcast_fusion
  174.2 1.1 broadcast_in_dim.60
  175.3 7.4 %all-to-all-start.2 = ((f32[32,256,32]{1,2,0:T(8,128)}), f32[32,256,32]{1,2,0:T(8,128)S(1)}, u32[]{:S(2)}, u32[]{:S(2)}) async-start(f32[32,256,32]{1,2,0:T(8,128)} %broadcast_in_dim.60), calls=%async_computation.2 | async-start | bytes 2097152 | tf_op jit(solution)/shard_map/all_to_all | solution.py:60
  182.7 0.7 fusion.59
  183.4 0.7 bitcast_dynamic-update-slice_fusion.1
  184.1 0.7 fusion.58
  184.7 48.1 %all-to-all-done.2 = f32[32,256,32]{1,2,0:T(8,128)S(1)} async-done(((f32[32,256,32]{1,2,0:T(8,128)}), f32[32,256,32]{1,2,0:T(8,128)S(1)}, u32[]{:S(2)}, u32[]{:S(2)}) %all-to-all-start.2) | async-done | bytes 1048608 | tf_op jit(solution)/shard_map/all_to_all | solution.py:60
  235.6 0.7 reshape.401
  236.3 7.2 %all-to-all-start.3 = ((f32[16,1,768]{2,1,0:T(1,128)}), f32[16,1,768]{2,1,0:T(1,128)S(1)}, u32[]{:S(2)}, u32[]{:S(2)}) async-start(f32[16,1,768]{2,1,0:T(1,128)} %reshape.401), calls=%async_computation.3 | async-start | bytes 98304 | tf_op jit(solution)/shard_map/all_to_all | solution.py:251
  244.2 13.9 %all-to-all-done.3 = f32[16,1,768]{2,1,0:T(1,128)S(1)} async-done(((f32[16,1,768]{2,1,0:T(1,128)}), f32[16,1,768]{2,1,0:T(1,128)S(1)}, u32[]{:S(2)}, u32[]{:S(2)}) %all-to-all-start.3) | async-done | bytes 49184 | tf_op jit(solution)/shard_map/all_to_all | solution.py:251
  258.0 0.7 reduce.10
  259.1 1.4 fusion.77
  261.2 1.1 copy.149
  262.2 2.8 %broadcast_in_dim.65 = f32[5,16,16,64,2]{2,1,4,3,0:T(8,128)} broadcast(f32[5,16,16,64]{2,1,3,0:T(8,128)S(1)} %copy.149), dimensions={0,1,2,3} | broadcast | bytes 983040 | tf_op jit(solution)/shard_map/broadcast_in_dim | solution.py:257
  265.0 3.3 %copy.150 = f32[1,5,16,16,128]{4,3,2,1,0:T(8,128)S(1)} copy(f32[1,5,16,16,128]{3,2,4,1,0:T(8,128)} %bitcast.170) | data formatting | bytes 1310720 | tf_op jit(solution)/shard_map/reshape | solution.py:257
  268.3 0.9 add.365
  (131 shorter events, 9.7 us)
Async XLA Ops:
  0.9 22.7 %collective-permute-start = (f32[16,16,128]{2,1,0:T(8,128)S(1)}, f32[16,16,128]{2,1,0:T(8,128)S(1)}, u32[]{:S(2)}, u32[]{:S(2)}) collective-permute-start(f32[16,16,128]{2,1,0:T(8,128)S(1)} %slice_bitcast_fusion.2), channel_id=1, source_target_pairs={{0,16},{16,32},{32,48},{48,64},{64,80},{80,96},{96,112},{112,128},... | collective-permute-start | bytes 393224 | tf_op jit(solution)/shard_map/ppermute | solution.py:17
  21.7 2.0 copy-start.2
  24.3 9.7 %copy-start = (f32[1,5,16,16,128]{4,3,2,1,0:T(8,128)S(1)}, f32[1,5,16,16,128]{4,3,2,1,0:T(8,128)}, u32[]{:S(2)}) copy-start(f32[1,5,16,16,128]{4,3,2,1,0:T(8,128)} %param.4) | copy-start | bytes 1966084
  34.1 35.1 %collective-permute-start.1 = (f32[6,5,16,128]{3,2,1,0:T(8,128)S(1)}, f32[6,5,16,128]{3,2,1,0:T(8,128)S(1)}, u32[]{:S(2)}, u32[]{:S(2)}) collective-permute-start(f32[6,5,16,128]{3,2,1,0:T(8,128)S(1)} %get-tuple-element.35), channel_id=1, source_target_pairs={{0,1},{1,2},{2,3},{3,4},{4,5},{5,6},{6,7},{7,8},{8,9},{9,10},{10,1... | collective-permute-start | bytes 737288 | tf_op jit(solution)/shard_map/ppermute | solution.py:27
  49.5 27.1 %collective-permute-start.2 = (f32[6,5,16,128]{3,2,1,0:T(8,128)S(1)}, f32[6,5,16,128]{3,2,1,0:T(8,128)S(1)}, u32[]{:S(2)}, u32[]{:S(2)}) collective-permute-start(f32[6,5,16,128]{3,2,1,0:T(8,128)S(1)} %get-tuple-element.36), channel_id=1, source_target_pairs={{1,0},{2,1},{3,2},{4,3},{5,4},{6,5},{7,6},{8,7},{9,8},{10,9},{11,1... | collective-permute-start | bytes 737288 | tf_op jit(solution)/shard_map/ppermute | solution.py:28
  77.8 0.9 copy-start.3
  149.6 22.6 %all-to-all-start.1 = ((f32[8,1,3072]{2,1,0:T(1,128)}), f32[8,1,3072]{2,1,0:T(1,128)S(1)}, u32[]{:S(2)}, u32[]{:S(2)}) async-start(f32[8,1,3072]{2,1,0:T(1,128)} %reshape.399), calls=%async_computation.1 | async-start | bytes 196608 | tf_op jit(solution)/shard_map/all_to_all | solution.py:48
  175.3 57.5 %all-to-all-start.2 = ((f32[32,256,32]{1,2,0:T(8,128)}), f32[32,256,32]{1,2,0:T(8,128)S(1)}, u32[]{:S(2)}, u32[]{:S(2)}) async-start(f32[32,256,32]{1,2,0:T(8,128)} %broadcast_in_dim.60), calls=%async_computation.2 | async-start | bytes 2097152 | tf_op jit(solution)/shard_map/all_to_all | solution.py:60
  236.3 24.1 %copy-start.4 = (f32[5,3,1,1]{0,1,3,2:T(4,128)S(1)}, f32[5,3,1,1]{0,1,3,2:T(4,128)}, u32[]{:S(2)}) copy-start(f32[5,3,1,1]{0,1,3,2:T(4,128)} %constant.174) | copy-start | bytes 184
  236.3 21.7 %all-to-all-start.3 = ((f32[16,1,768]{2,1,0:T(1,128)}), f32[16,1,768]{2,1,0:T(1,128)S(1)}, u32[]{:S(2)}, u32[]{:S(2)}) async-start(f32[16,1,768]{2,1,0:T(1,128)} %reshape.401), calls=%async_computation.3 | async-start | bytes 98304 | tf_op jit(solution)/shard_map/all_to_all | solution.py:251
  265.0 3.3 %copy-start.1 = (f32[1,5,16,16,128]{4,3,2,1,0:T(8,128)S(1)}, f32[1,5,16,16,128]{4,3,2,1,0:T(8,128)}, u32[]{:S(2)}) copy-start(f32[1,5,16,16,128]{4,3,2,1,0:T(8,128)} %bitcast_dynamic-update-slice_fusion) | copy-start | bytes 1966084
